TPU v7x, 512 devices: a whole 4x8x8 slice. The times are simulated.
512 devices in a mesh: elem: 32 (over x, y_lo, core), basis: 16 (over z, y_hi).
Axes of the slice: x: 4, y: 8 (y_hi: 2, y_lo: 4; y = y_hi * 4 + y_lo), z: 8, core: 2. Of those that a mesh axis runs over, the one named last changes fastest.
Arguments:
- basis_vals: bfloat16 [64, 60, 46656], P('elem', None, 'basis'), may hold values from -6 to 6
- basis_grad: bfloat16 [64, 3, 60, 46656], P('elem', None, None, 'basis'), may hold values from -6 to 6
- potential: float32 [64, 46656], P('elem', 'basis'), may hold values from -12 to 12
- face_traces: bfloat16 [64, 2, 2, 60, 1296], P('elem', None, None, None, 'basis'), may hold values from -6 to 6
- penalty: float32 [64], replicated, may hold values from 4 to 40
- orientation: int32 [64], replicated, may hold values from 0 to 1
Outputs:
- blocks: float32 [64, 2, 3600], P('elem', None, 'basis')
All inputs are finite; a program needn't handle non-finite values.
Results may differ from a plain program's by a relative error of at most 0.0003.
Values may be sent and summed in bfloat16 or wider, within the bound.
No kernel may reach another device: no remote copies, remote signals or barrier semaphores. Data moves between devices by JAX's collectives and lax.ppermute only.
A program may use at most 64 MiB of HBM per device.

v0:
```python
import jax
import jax.numpy as jnp
from jax import lax
from jax.sharding import PartitionSpec as P

PTS = 46656
FP = 1296


def from_behind(value, axis, steps):
    count = lax.axis_size(axis)
    pairs = [(source, (source + steps) % count) for source in range(count)]
    return lax.ppermute(value, axis, pairs)


def orient(face_traces, codes):
    flag = (codes == 0)[:, None, None, None]
    upper = jnp.where(flag, face_traces[:, 1], face_traces[:, 0])
    lower = jnp.where(flag, face_traces[:, 0], face_traces[:, 1])
    sign = (1 - 2 * codes).astype(jnp.bfloat16)[:, None, None]
    return (upper[:, 0], upper[:, 1] * sign, lower[:, 0], lower[:, 1] * sign)


def face_gram(left, right):
    return jnp.einsum("eaq,ebq->eab", left, right, preferred_element_type=jnp.float32)


def on_device(basis_vals, basis_grad, potential, face_traces, penalty, orientation):
    local_count, width, points = basis_vals.shape
    start = lax.axis_index("elem") * local_count
    codes = lax.dynamic_slice_in_dim(orientation, start, local_count)
    upper_all = 0.5 * (penalty + jnp.roll(penalty, -1))
    lower_all = 0.5 * (jnp.roll(penalty, 1) + penalty)
    upper_pen = lax.dynamic_slice_in_dim(upper_all, start, local_count)[:, None, None]
    lower_pen = lax.dynamic_slice_in_dim(lower_all, start, local_count)[:, None, None]
    vp, dp, vm, dm = orient(face_traces, codes)
    weighted = (basis_vals.astype(jnp.float32) * potential[:, None, :] * (1.0 / PTS)).astype(
        jnp.bfloat16
    )
    volume = jnp.einsum("eap,ebp->eab", weighted, basis_vals, preferred_element_type=jnp.float32)
    kinetic = jnp.einsum(
        "ecap,ecbp->eab", basis_grad, basis_grad, preferred_element_type=jnp.float32
    )
    own = (
        -0.25 * (face_gram(dp, vp) + face_gram(vp, dp))
        + upper_pen * face_gram(vp, vp)
        + 0.25 * (face_gram(dm, vm) + face_gram(vm, dm))
        + lower_pen * face_gram(vm, vm)
    )
    diag = volume + 0.5 / PTS * kinetic + own * (1.0 / FP)
    diag = 0.5 * (diag + jnp.swapaxes(diag, 1, 2))
    flat = width * width
    sent = jnp.stack([vm[0], dm[0]])
    arrived = from_behind(sent, "elem", -1)
    vm_next = jnp.concatenate([vm[1:], arrived[0][None]], axis=0)
    dm_next = jnp.concatenate([dm[1:], arrived[1][None]], axis=0)
    pair = (
        0.25 * (face_gram(dp, vm_next) - face_gram(vp, dm_next))
        - upper_pen * face_gram(vp, vm_next)
    ) * (1.0 / FP)
    diag_flat = diag.reshape(local_count, flat)
    pair_flat = pair.reshape(local_count, flat)
    terms = jnp.stack([diag_flat, pair_flat], axis=1)
    summed = lax.psum_scatter(terms, "basis", scatter_dimension=2, tiled=True)
    return summed


def solution(mesh):
    in_specs = (
        P("elem", None, "basis"),
        P("elem", None, None, "basis"),
        P("elem", "basis"),
        P("elem", None, None, None, "basis"),
        P(),
        P(),
    )
    out_specs = P("elem", None, "basis")
    return jax.shard_map(
        on_device, mesh=mesh, in_specs=in_specs, out_specs=out_specs, check_vma=False
    )
```

profile of v0, /device:TPU:6, one launch (start us, length us, event | category | flops | bytes accessed | tf_op | source)
XLA Modules:
  0.0 124.2 jit_solution(11426896644082988591)
XLA Ops:
  0.0 0.7 broadcast_compare_fusion
  0.7 0.7 subtract_convert_fusion
  1.5 0.9 fusion.41
  2.4 0.1 fusion.20
  2.5 0.1 fusion.22
  2.6 5.2 %collective-permute-start = (bf16[2,60,81]{2,1,0:T(8,128)(2,1)S(1)}, bf16[2,60,81]{2,1,0:T(8,128)(2,1)S(1)}, u32[]{:S(2)}, u32[]{:S(2)}) collective-permute-start(bf16[2,60,81]{2,1,0:T(8,128)(2,1)S(1)} %pad_maximum_fusion.1), channel_id=1, source_target_pairs={{0,496},{16,0},{32,16},{48,32},{64,48},{80,64},{96,80},{112,96},{1... | collective-permute-start | bytes 58328 | tf_op jit(solution)/shard_map/ppermute | solution.py:13
  7.8 0.1 bitcast_select_fusion
  7.9 0.8 fusion.45
  8.7 1.3 %fusion.44 = (f32[1]{0:T(128)}, f32[1]{0:T(128)}) fusion(f32[64]{0:T(128)} %param.10), kind=kLoop, calls=%fused_computation.63 | loop fusion | bytes 16 | tf_op jit(solution)/shard_map/jit(_roll_static)/slice | solution.py:33
  10.0 0.0 copy-start
  10.0 0.0 copy-start.1
  10.0 0.1 fusion.28
  10.2 2.0 %fusion.37 = (f32[64]{0:T(128)S(1)}, f32[64]{0:T(128)S(1)}) fusion(f32[64]{0:T(128)} %param.10, f32[63]{0:T(128)S(1)} %get-tuple-element.17, f32[1]{0:T(128)} %get-tuple-element.15, f32[1]{0:T(128)} %get-tuple-element.16, f32[63]{0:T(128)S(1)} %get-tuple-element.18), kind=kLoop, calls=%fused_computation.53 | loop fusion | flops 384 | bytes 1280 | tf_op jit(solution)/shard_map/mul | solution.py:33
  12.2 0.1 dynamic_slice.10
  12.3 0.2 fusion.31
  12.4 0.2 fusion.14
  12.7 0.1 dynamic_slice.11
  12.7 3.0 %fusion.15 = f32[2,60,60]{2,1,0:T(8,128)S(1)} fusion(bf16[2,3,60,2916]{3,0,2,1:T(2,128)(2,1)} %param.7), kind=kOutput, calls=%fused_computation.21 | convolution fusion | flops 125978400 | bytes 2128320 | tf_op jit(solution)/shard_map/ecap,ecbp->eab/dot_general | solution.py:41
  15.8 0.1 fusion.13
  15.9 0.1 fusion.12
  16.1 0.1 fusion.10
  16.2 0.0 copy-done
  16.2 0.0 copy-done.1
  16.3 0.7 multiply_convert_fusion
  17.0 0.4 fusion.2
  17.4 0.1 copy.39
  17.5 0.1 copy.40
  17.6 0.1 stack_reshape.6
  17.7 1.3 %dynamic-slice = u32[1]{0:T(128)} dynamic-slice(u32[512]{0:T(512)} %constant.35, u32[]{:T(128)S(6)} %add.75), dynamic_slice_sizes={1} | dynamic-slice | bytes 12
  19.7 0.0 collective-permute-done
  19.7 0.1 fusion.24
  19.8 0.2 fusion.8
  20.0 0.1 fusion.7
  20.2 0.1 stack_reshape.7
  20.3 103.2 %all-reduce = f32[2,2,3600]{2,0,1:T(2,128)S(1)} all-reduce(f32[2,2,3600]{2,0,1:T(2,128)S(1)} %pad_maximum_fusion), channel_id=2, replica_groups=mesh['elem'=32,'basis'=16] {'basis'}, use_global_device_ids=true, to_apply=%region_0.1.clone | all-reduce | flops 14400 | bytes 115200
  123.5 0.1 constant_dynamic-slice_fusion
  123.6 0.6 copy.41
  (6 shorter events, 0.1 us)
Async XLA Ops:
  2.6 17.1 %collective-permute-start = (bf16[2,60,81]{2,1,0:T(8,128)(2,1)S(1)}, bf16[2,60,81]{2,1,0:T(8,128)(2,1)S(1)}, u32[]{:S(2)}, u32[]{:S(2)}) collective-permute-start(bf16[2,60,81]{2,1,0:T(8,128)(2,1)S(1)} %pad_maximum_fusion.1), channel_id=1, source_target_pairs={{0,496},{16,0},{32,16},{48,32},{64,48},{80,64},{96,80},{112,96},{1... | collective-permute-start | bytes 58328 | tf_op jit(solution)/shard_map/ppermute | solution.py:13
  10.0 6.2 %copy-start = (bf16[2,60,2916]{2,0,1:T(2,128)(2,1)S(1)}, bf16[2,60,2916]{2,0,1:T(2,128)(2,1)}, u32[]{:S(2)}) copy-start(bf16[2,60,2916]{2,0,1:T(2,128)(2,1)} %param.6) | copy-start | bytes 2099524
  10.0 6.2 %copy-start.1 = (f32[2,2916]{1,0:T(2,128)S(1)}, f32[2,2916]{1,0:T(2,128)}, u32[]{:S(2)}) copy-start(f32[2,2916]{1,0:T(2,128)} %param.8) | copy-start | bytes 69988
where the time goes:
time: 124 us
  blocking collectives  103 us (83%)
  local copies, waits for them, and re-layouts  5.63 us (5%)
  starting transfers between devices  5.21 us (4%)
  matrix products  4.84 us (4%)
  other arithmetic  4.51 us (4%)
    unnamed x1, blocking collectives  103 us
    ppermute x1, starting transfers between devices, from_behind(): return lax.ppermute(value, axis, pairs)  5.21 us
    dot_general x1, matrix products, on_device(): jnp.einsum('ecap,ecbp->eab', basis_grad, basis_grad, preferred_element_ty...  3.04 us
  transfers between devices with their start and end apart: 1, of which 0 were waited for; matrix products, arithmetic and copies ran while one was open for 9% of the time, Pallas kernels for 0%

commit v1 on v0

v1 whole, which is shorter than its diff:
```python
import jax
import jax.numpy as jnp
from jax import lax
from jax.experimental import pallas as pl
from jax.experimental.pallas import tpu as pltpu
from jax.sharding import PartitionSpec as P

PTS = 46656
FP = 1296
LANES = 128
NT = (((1,), (1,)), ((), ()))
MIB = 1024 * 1024


def gram(left, right):
    return lax.dot_general(left, right, NT, preferred_element_type=jnp.float32)


def merged(value):
    rows, pair, lanes = value.shape
    return value.reshape(rows * pair, lanes)


def parities(size):
    shape = (size, size)
    row = lax.broadcasted_iota(jnp.int32, shape, 0) % 2
    col = lax.broadcasted_iota(jnp.int32, shape, 1) % 2
    return row, col


def fold(first, second, stage, turned, width):
    size = first.shape[0]
    half = size // 2
    stage[0] = first
    stage[1] = second
    rows = [stage[n, pl.ds(0, half, stride=2), :] + stage[n, pl.ds(1, half, stride=2), :] for n in range(2)]
    turned[...] = jnp.concatenate(rows, axis=0).T
    both = turned[pl.ds(0, half, stride=2), :] + turned[pl.ds(1, half, stride=2), :]
    return both[:width, :width], both[:width, half : half + width]


def local_terms(grad, vals, pot, faces, penalty, orientation, diag, cross, scales, edge, grads, tiles, pots, sides,
                pens, codes, stage, turned, sems):
    comps, width, count, points = grad.shape
    even = points // LANES * LANES
    rows = width * count

    moves = [
        pltpu.make_async_copy(source, target, sems.at[comps + n])
        for n, (source, target) in enumerate(
            ((penalty, pens), (orientation, codes), (faces, sides), (pot, pots), (vals, tiles))
        )
    ]

    def grad_move(comp):
        return pltpu.make_async_copy(grad.at[comp], grads.at[comp], sems.at[comp])

    for move in moves:
        move.start()
    for comp in range(comps):
        grad_move(comp).start()
    for move in moves[:3]:
        move.wait()

    first = lax.axis_index("elem") * count
    total = penalty.shape[0]
    row, col = parities(rows)

    def code_at(element):
        return codes[lax.rem(first + element, total)]

    def sign_of(code):
        return (1 - 2 * code).astype(jnp.float32)

    def pen_between(element):
        left = pens[lax.rem(first + element + total - 1, total)]
        return 0.5 * (left + pens[lax.rem(first + element, total)])

    uppers = [merged(sides[element, 1 - code_at(element)]) for element in range(count)]
    lowers = [merged(sides[element, code_at(element)]) for element in range(count)]

    def face_part(element):
        mixed = jnp.where(row != col, 0.25 * sign_of(code_at(element)), 0.0)
        both = row + col == 0
        upper_scale = jnp.where(both, pen_between(element + 1), -mixed)
        lower_scale = jnp.where(both, pen_between(element), mixed)
        upper, lower = uppers[element], lowers[element]
        return (upper_scale * gram(upper, upper) + lower_scale * gram(lower, lower)) * (1.0 / FP)

    def cross_scale(element):
        upper_sign, lower_sign = sign_of(code_at(element)), sign_of(code_at(element + 1))
        return (1.0 / FP) * jnp.where(
            row == 0,
            jnp.where(col == 0, -pen_between(element + 1), 0.25 * upper_sign),
            jnp.where(col == 0, -0.25 * lower_sign, 0.0),
        )

    cross[...] = cross_scale(0) * gram(lowers[1], uppers[0])
    edge[...] = uppers[count - 1]
    scale = cross_scale(count - 1)
    for side in range(2):
        scales[side] = jnp.where(code_at(count) == side, scale, 0.0)
    face_parts = [face_part(element) for element in range(count)]

    for move in moves[3:]:
        move.wait()
    odd = lax.broadcasted_iota(jnp.int32, (rows, LANES), 0) % 2 == 1

    def weighted(tile, level):
        level = jnp.where(odd[:, : tile.shape[1]], level[1:2], level[0:1])
        return (tile.astype(jnp.float32) * level * (1.0 / PTS)).astype(jnp.bfloat16)

    tile = merged(tiles[:, :, :even])
    parts = [weighted(tile[:, at : at + LANES], pots[:, at : at + LANES]) for at in range(0, even, LANES)]
    end = merged(tiles[:, :, even:])
    volume = gram(jnp.concatenate(parts, axis=1), tile) + gram(weighted(end, pots[:, even:]), end)

    def add_comp(comp, kinetic):
        grad_move(comp).wait()
        slope = merged(grads[comp, :, :, :even])
        end = merged(grads[comp, :, :, even:])
        return kinetic + gram(slope, slope) + gram(end, end)

    kinetic = lax.fori_loop(0, comps, add_comp, jnp.zeros((rows, rows), jnp.float32))
    inner = 0.5 * (volume + volume.T) + (0.5 / PTS) * kinetic
    parts = [
        jnp.where((row == element) & (col == element), inner, 0.0) + face_parts[element] for element in range(count)
    ]
    diag[0], diag[1] = fold(*parts, stage, turned, width)


def pair_terms(arrived, edge, cross, scales, diag, out, stage, turned, rows):
    width = diag.shape[1]
    share = out.shape[2]
    upper = edge[...]
    parts = [gram(merged(arrived[0, side]), upper) * scales[side] for side in range(2)]
    pairs = fold(cross[...], parts[0] + parts[1], stage, turned, width)
    kinds = 2 * len(pairs)
    for element, pair in enumerate(pairs):
        rows[pl.ds(2 * element, width, stride=kinds), :] = diag[element]
        rows[pl.ds(2 * element + 1, width, stride=kinds), :] = pair
    for slot, owner in enumerate(exchange_order(out.shape[0])):
        at, end = owner * share, (owner + 1) * share
        pieces = []
        while at < end:
            row, col = divmod(at, width)
            size = min(width - col, end - at)
            pieces.append(rows[pl.ds(kinds * row, kinds), pl.ds(col, size)])
            at += size
        out[slot] = jnp.concatenate(pieces, axis=1)


def exchange_order(ways):
    return [(slot + ways * 11 // 16) % ways for slot in range(ways)]


def total_terms(shared, out):
    total = jnp.sum(shared[...], axis=0)
    for element in range(out.shape[0]):
        out[element] = total[2 * element : 2 * element + 2]


def from_behind(value, axis, steps):
    count = lax.axis_size(axis)
    pairs = [(source, (source + steps) % count) for source in range(count)]
    return lax.ppermute(value, axis, pairs)


def on_device(basis_vals, basis_grad, potential, face_traces, penalty, orientation):
    count, width, points = basis_vals.shape
    comps = basis_grad.shape[1]
    face_points = face_traces.shape[-1]
    faces = face_traces.transpose(0, 1, 3, 2, 4)
    arrived = from_behind(faces, "elem", -1)
    grad = basis_grad.transpose(1, 2, 0, 3)
    vals = basis_vals.transpose(1, 0, 2)
    held = (grad, vals, potential, faces, penalty, orientation)
    held = [pltpu.with_memory_space_constraint(array, pltpu.HBM) for array in held]
    rows = width * count
    any_space = pl.BlockSpec(memory_space=pl.ANY)
    in_vmem = pl.BlockSpec(memory_space=pltpu.VMEM)
    fold_scratch = [pltpu.VMEM((2, rows, rows), jnp.float32), pltpu.VMEM((rows, rows), jnp.float32)]
    diag, cross, scales, edge = pl.pallas_call(
        local_terms,
        out_shape=[
            pltpu.VMEM((count, width, width), jnp.float32),
            pltpu.VMEM((rows, rows), jnp.float32),
            pltpu.VMEM((2, rows, rows), jnp.float32),
            pltpu.VMEM((rows, face_points), jnp.bfloat16),
        ],
        in_specs=[any_space] * 6,
        out_specs=[in_vmem] * 4,
        scratch_shapes=[
            pltpu.VMEM(grad.shape, jnp.bfloat16),
            pltpu.VMEM(vals.shape, jnp.bfloat16),
            pltpu.VMEM(potential.shape, jnp.float32),
            pltpu.VMEM(faces.shape, jnp.bfloat16),
            pltpu.SMEM(penalty.shape, jnp.float32),
            pltpu.SMEM(orientation.shape, jnp.int32),
            *fold_scratch,
            pltpu.SemaphoreType.DMA((comps + 5,)),
        ],
        compiler_params=pltpu.CompilerParams(vmem_limit_bytes=16 * MIB),
        cost_estimate=pl.CostEstimate(flops=400_000_000, bytes_accessed=3_000_000, transcendentals=0),
        name="local_terms",
    )(*held)
    ways = lax.axis_size("basis")
    share = width * width // ways
    terms = pl.pallas_call(
        pair_terms,
        out_shape=pltpu.VMEM((ways, 2 * count, share), jnp.float32),
        in_specs=[in_vmem] * 5,
        out_specs=in_vmem,
        scratch_shapes=[*fold_scratch, pltpu.VMEM((2 * count * width, width), jnp.float32)],
        compiler_params=pltpu.CompilerParams(vmem_limit_bytes=8 * MIB),
        name="pair_terms",
    )(pltpu.with_memory_space_constraint(arrived, pltpu.VMEM), edge, cross, scales, diag)
    shared = lax.all_to_all(terms, "basis", 0, 0, axis_index_groups=[exchange_order(ways)])
    return pl.pallas_call(
        total_terms,
        out_shape=jax.ShapeDtypeStruct((count, 2, share), jnp.float32),
        in_specs=[in_vmem],
        out_specs=in_vmem,
        compiler_params=pltpu.CompilerParams(vmem_limit_bytes=8 * MIB),
        name="total_terms",
    )(pltpu.with_memory_space_constraint(shared, pltpu.VMEM))


def solution(mesh):
    in_specs = (
        P("elem", None, "basis"),
        P("elem", None, None, "basis"),
        P("elem", "basis"),
        P("elem", None, None, None, "basis"),
        P(),
        P(),
    )
    out_specs = P("elem", None, "basis")
    return jax.shard_map(
        on_device, mesh=mesh, in_specs=in_specs, out_specs=out_specs, check_vma=False
    )
```

time: 124 us -> 33.4 us (0.27)
  the two profiles are of different devices: /device:TPU:6 before, /device:TPU:63 now
where the time goes in v1:
time: 33.4 us; the launch traced here: 33.2 us
  blocking collectives  21.8 us (65%)
  Pallas kernels  5.35 us (16%)
  waiting for transfers between devices  3.46 us (10%)
  starting transfers between devices  2.57 us (8%)
    all_to_all x1, blocking collectives, on_device(): lax.all_to_all(terms, 'basis', 0, 0, axis_index_groups=[exchange_order(wa...  21.8 us
    pallas_call x1, Pallas kernels, on_device(): pl.pallas_call(local_terms, out_shape=[pltpu.VMEM((count, width, width),...  4.26 us
    ppermute x1, waiting for transfers between devices, from_behind(): return lax.ppermute(value, axis, pairs)  3.46 us
    ppermute x1, starting transfers between devices, from_behind(): return lax.ppermute(value, axis, pairs)  2.57 us
  transfers between devices with their start and end apart: 1, of which 1 were waited for; matrix products, arithmetic and copies ran while one was open for 0% of the time, Pallas kernels for 13%

profile of v1, /device:TPU:63, one launch (start us, length us, event | category | flops | bytes accessed | tf_op | source)
XLA Modules:
  0.0 33.2 jit_solution(16199128199700356519)
XLA Ops:
  0.0 2.6 %collective-permute-start = (bf16[2,2,60,2,81]{4,3,2,1,0:T(2,128)(2,1)}, bf16[2,2,60,2,81]{4,3,2,1,0:T(2,128)(2,1)S(1)}, u32[]{:S(2)}, u32[]{:S(2)}) collective-permute-start(bf16[2,2,60,2,81]{4,3,2,1,0:T(2,128)(2,1)} %bitcast.5), channel_id=1, source_target_pairs={{0,496},{16,0},{32,16},{48,32},{64,48},{80,64},{96,80},{112,96},{1... | collective-permute-start | bytes 233288 | tf_op jit(solution)/shard_map/ppermute | solution.py:166
  2.6 4.3 %local_terms.1 = (f32[2,60,60]{2,1,0:T(8,128)S(1)}, f32[120,120]{1,0:T(8,128)S(1)}, f32[2,120,120]{2,1,0:T(8,128)S(1)}, bf16[120,81]{1,0:T(8,128)(2,1)S(1)}) custom-call(bf16[3,60,2,2916]{3,2,1,0:T(2,128)(2,1)} %bitcast.3, bf16[60,2,2916]{2,1,0:T(2,128)(2,1)} %bitcast.4, f32[2,2916]{1,0:T(2,128)} %pot.1, bf16[2,2,60,2,81]{4,3,2,1,0:T(2,128)(2,1)} %bitcast.6, ...), custom_call_target="tpu_custom_call" | custom-call | flops 400000000 | bytes 3000000 | tf_op jit(solution)/shard_map/local_terms/pallas_call | solution.py:183
  6.8 3.5 %collective-permute-done.arrived = bf16[2,2,60,2,81]{4,3,2,1,0:T(2,128)(2,1)S(1)} collective-permute-done((bf16[2,2,60,2,81]{4,3,2,1,0:T(2,128)(2,1)}, bf16[2,2,60,2,81]{4,3,2,1,0:T(2,128)(2,1)S(1)}, u32[]{:S(2)}, u32[]{:S(2)}) %collective-permute-start) | collective-permute-done | bytes 77792 | tf_op jit(solution)/shard_map/ppermute | solution.py:166
  10.3 0.5 %pair_terms.1 = f32[16,4,225]{2,1,0:T(4,128)S(1)} custom-call(bf16[2,2,60,2,81]{4,3,2,1,0:T(2,128)(2,1)S(1)} %collective-permute-done.arrived, bf16[120,81]{1,0:T(8,128)(2,1)S(1)} %get-tuple-element.9.edge, f32[120,120]{1,0:T(8,128)S(1)} %get-tuple-element.10.cross, f32[2,120,120]{2,1,0:T(8,128)S(1)} %get-tuple-element.11.scales, ...), custom_call_target="tpu_custom_call" | custom-call | tf_op jit(solution)/shard_map/pair_terms/pallas_call | solution.py:209
  10.8 21.8 %all_to_all.5.shared = f32[16,4,225]{2,1,0:T(4,128)S(1)} all-to-all(f32[16,4,225]{2,1,0:T(4,128)S(1)} %pair_terms.1), channel_id=1, replica_groups={{11,12,13,14,15,0,1,2,3,4,5,6,7,8,9,10},{27,28,29,30,31,16,17,18,19,20,..., dimensions={0} | all-to-all | bytes 115200 | tf_op jit(solution)/shard_map/all_to_all | solution.py:218
  32.6 0.6 %total_terms.1 = f32[2,2,225]{2,1,0:T(2,128)} custom-call(f32[16,4,225]{2,1,0:T(4,128)S(1)} %all_to_all.5.shared), custom_call_target="tpu_custom_call" | custom-call | tf_op jit(solution)/shard_map/total_terms/pallas_call | solution.py:219
Async XLA Ops:
  0.0 10.3 %collective-permute-start = (bf16[2,2,60,2,81]{4,3,2,1,0:T(2,128)(2,1)}, bf16[2,2,60,2,81]{4,3,2,1,0:T(2,128)(2,1)S(1)}, u32[]{:S(2)}, u32[]{:S(2)}) collective-permute-start(bf16[2,2,60,2,81]{4,3,2,1,0:T(2,128)(2,1)} %bitcast.5), channel_id=1, source_target_pairs={{0,496},{16,0},{32,16},{48,32},{64,48},{80,64},{96,80},{112,96},{1... | collective-permute-start | bytes 233288 | tf_op jit(solution)/shard_map/ppermute | solution.py:166

commit v2 on v1

--- a/solution.py
+++ b/solution.py
@@ -42,7 +42,6 @@
 def local_terms(grad, vals, pot, faces, penalty, orientation, diag, cross, scales, edge, grads, tiles, pots, sides,
                 pens, codes, stage, turned, sems):
     comps, width, count, points = grad.shape
-    even = points // LANES * LANES
     rows = width * count
 
     moves = [
@@ -55,9 +54,12 @@
     def grad_move(comp):
         return pltpu.make_async_copy(grad.at[comp], grads.at[comp], sems.at[comp])
 
-    for move in moves:
+    for move in moves[:3]:
         move.start()
-    for comp in range(comps):
+    grad_move(0).start()
+    for move in moves[3:]:
+        move.start()
+    for comp in range(1, comps):
         grad_move(comp).start()
     for move in moves[:3]:
         move.wait()
@@ -102,26 +104,31 @@
         scales[side] = jnp.where(code_at(count) == side, scale, 0.0)
     face_parts = [face_part(element) for element in range(count)]
 
-    for move in moves[3:]:
-        move.wait()
     odd = lax.broadcasted_iota(jnp.int32, (rows, LANES), 0) % 2 == 1
 
     def weighted(tile, level):
         level = jnp.where(odd[:, : tile.shape[1]], level[1:2], level[0:1])
         return (tile.astype(jnp.float32) * level * (1.0 / PTS)).astype(jnp.bfloat16)
 
-    tile = merged(tiles[:, :, :even])
-    parts = [weighted(tile[:, at : at + LANES], pots[:, at : at + LANES]) for at in range(0, even, LANES)]
-    end = merged(tiles[:, :, even:])
-    volume = gram(jnp.concatenate(parts, axis=1), tile) + gram(weighted(end, pots[:, even:]), end)
-
-    def add_comp(comp, kinetic):
+    volume, kinetic = [], []
+    half = points // LANES // 2 * LANES
+    spans = ((0, half), (half, points))
+    for comp in range(comps):
         grad_move(comp).wait()
-        slope = merged(grads[comp, :, :, :even])
-        end = merged(grads[comp, :, :, even:])
-        return kinetic + gram(slope, slope) + gram(end, end)
-
-    kinetic = lax.fori_loop(0, comps, add_comp, jnp.zeros((rows, rows), jnp.float32))
+        for at, end in spans:
+            slope = merged(grads[comp, :, :, at:end])
+            kinetic.append(gram(slope, slope))
+        if comp == 0:
+            for move in moves[3:]:
+                move.wait()
+            for at, end in spans:
+                tile = merged(tiles[:, :, at:end])
+                parts = [
+                    weighted(tile[:, n - at : min(n + LANES, end) - at], pots[:, n : min(n + LANES, end)])
+                    for n in range(at, end, LANES)
+                ]
+                volume.append(gram(jnp.concatenate(parts, axis=1), tile))
+    volume, kinetic = sum(volume), sum(kinetic)
     inner = 0.5 * (volume + volume.T) + (0.5 / PTS) * kinetic
     parts = [
         jnp.where((row == element) & (col == element), inner, 0.0) + face_parts[element] for element in range(count)

time: 33.4 us -> 33.4 us (level)
  the two profiles are of different devices: /device:TPU:63 before, /device:TPU:32 now
where the time goes in v2:
time: 33.4 us; the launch traced here: 33.3 us
  blocking collectives  23.3 us (70%)
  Pallas kernels  5.54 us (17%)
  starting transfers between devices  4.43 us (13%)
    all_to_all x1, blocking collectives, on_device(): lax.all_to_all(terms, 'basis', 0, 0, axis_index_groups=[exchange_order(wa...  23.3 us
    pallas_call x1, Pallas kernels, on_device(): pl.pallas_call(local_terms, out_shape=[pltpu.VMEM((count, width, width),...  4.46 us
    ppermute x1, starting transfers between devices, from_behind(): return lax.ppermute(value, axis, pairs)  4.43 us
  transfers between devices with their start and end apart: 1, of which 0 were waited for; matrix products, arithmetic and copies ran while one was open for 0% of the time, Pallas kernels for 13%

profile of v2, /device:TPU:32, one launch (start us, length us, event | category | flops | bytes accessed | tf_op | source)
XLA Modules:
  0.0 33.3 jit_solution(7838481172207500497)
XLA Ops:
  0.0 4.4 %collective-permute-start = (bf16[2,2,60,2,81]{4,3,2,1,0:T(2,128)(2,1)}, bf16[2,2,60,2,81]{4,3,2,1,0:T(2,128)(2,1)S(1)}, u32[]{:S(2)}, u32[]{:S(2)}) collective-permute-start(bf16[2,2,60,2,81]{4,3,2,1,0:T(2,128)(2,1)} %bitcast.5), channel_id=1, source_target_pairs={{0,496},{16,0},{32,16},{48,32},{64,48},{80,64},{96,80},{112,96},{1... | collective-permute-start | bytes 233288 | tf_op jit(solution)/shard_map/ppermute | solution.py:173
  4.4 4.5 %local_terms.1 = (f32[2,60,60]{2,1,0:T(8,128)S(1)}, f32[120,120]{1,0:T(8,128)S(1)}, f32[2,120,120]{2,1,0:T(8,128)S(1)}, bf16[120,81]{1,0:T(8,128)(2,1)S(1)}) custom-call(bf16[3,60,2,2916]{3,2,1,0:T(2,128)(2,1)} %bitcast.3, bf16[60,2,2916]{2,1,0:T(2,128)(2,1)} %bitcast.4, f32[2,2916]{1,0:T(2,128)} %pot.1, bf16[2,2,60,2,81]{4,3,2,1,0:T(2,128)(2,1)} %bitcast.6, ...), custom_call_target="tpu_custom_call" | custom-call | flops 400000000 | bytes 3000000 | tf_op jit(solution)/shard_map/local_terms/pallas_call | solution.py:190
  8.9 0.0 collective-permute-done.arrived
  8.9 0.5 %pair_terms.1 = f32[16,4,225]{2,1,0:T(4,128)S(1)} custom-call(bf16[2,2,60,2,81]{4,3,2,1,0:T(2,128)(2,1)S(1)} %collective-permute-done.arrived, bf16[120,81]{1,0:T(8,128)(2,1)S(1)} %get-tuple-element.9.edge, f32[120,120]{1,0:T(8,128)S(1)} %get-tuple-element.10.cross, f32[2,120,120]{2,1,0:T(8,128)S(1)} %get-tuple-element.11.scales, ...), custom_call_target="tpu_custom_call" | custom-call | tf_op jit(solution)/shard_map/pair_terms/pallas_call | solution.py:216
  9.4 23.3 %all_to_all.5.shared = f32[16,4,225]{2,1,0:T(4,128)S(1)} all-to-all(f32[16,4,225]{2,1,0:T(4,128)S(1)} %pair_terms.1), channel_id=1, replica_groups={{11,12,13,14,15,0,1,2,3,4,5,6,7,8,9,10},{27,28,29,30,31,16,17,18,19,20,..., dimensions={0} | all-to-all | bytes 115200 | tf_op jit(solution)/shard_map/all_to_all | solution.py:225
  32.7 0.6 %total_terms.1 = f32[2,2,225]{2,1,0:T(2,128)} custom-call(f32[16,4,225]{2,1,0:T(4,128)S(1)} %all_to_all.5.shared), custom_call_target="tpu_custom_call" | custom-call | tf_op jit(solution)/shard_map/total_terms/pallas_call | solution.py:226
Async XLA Ops:
  0.0 8.9 %collective-permute-start = (bf16[2,2,60,2,81]{4,3,2,1,0:T(2,128)(2,1)}, bf16[2,2,60,2,81]{4,3,2,1,0:T(2,128)(2,1)S(1)}, u32[]{:S(2)}, u32[]{:S(2)}) collective-permute-start(bf16[2,2,60,2,81]{4,3,2,1,0:T(2,128)(2,1)} %bitcast.5), channel_id=1, source_target_pairs={{0,496},{16,0},{32,16},{48,32},{64,48},{80,64},{96,80},{112,96},{1... | collective-permute-start | bytes 233288 | tf_op jit(solution)/shard_map/ppermute | solution.py:173

commit v3 on v1

--- a/solution.py
+++ b/solution.py
@@ -16,9 +16,9 @@
     return lax.dot_general(left, right, NT, preferred_element_type=jnp.float32)
 
 
-def merged(value):
-    rows, pair, lanes = value.shape
-    return value.reshape(rows * pair, lanes)
+def merged(array):
+    *lead, rows, pair, lanes = array.shape
+    return array.reshape(*lead, rows * pair, lanes)
 
 
 def parities(size):
@@ -48,12 +48,12 @@
     moves = [
         pltpu.make_async_copy(source, target, sems.at[comps + n])
         for n, (source, target) in enumerate(
-            ((penalty, pens), (orientation, codes), (faces, sides), (pot, pots), (vals, tiles))
+            ((penalty, pens), (orientation, codes), (merged(faces), sides), (pot, pots), (merged(vals), tiles))
         )
     ]
 
     def grad_move(comp):
-        return pltpu.make_async_copy(grad.at[comp], grads.at[comp], sems.at[comp])
+        return pltpu.make_async_copy(merged(grad).at[comp], grads.at[comp], sems.at[comp])
 
     for move in moves:
         move.start()
@@ -76,8 +76,8 @@
         left = pens[lax.rem(first + element + total - 1, total)]
         return 0.5 * (left + pens[lax.rem(first + element, total)])
 
-    uppers = [merged(sides[element, 1 - code_at(element)]) for element in range(count)]
-    lowers = [merged(sides[element, code_at(element)]) for element in range(count)]
+    uppers = [sides[element, 1 - code_at(element)] for element in range(count)]
+    lowers = [sides[element, code_at(element)] for element in range(count)]
 
     def face_part(element):
         mixed = jnp.where(row != col, 0.25 * sign_of(code_at(element)), 0.0)
@@ -110,15 +110,15 @@
         level = jnp.where(odd[:, : tile.shape[1]], level[1:2], level[0:1])
         return (tile.astype(jnp.float32) * level * (1.0 / PTS)).astype(jnp.bfloat16)
 
-    tile = merged(tiles[:, :, :even])
+    tile = tiles[:, :even]
     parts = [weighted(tile[:, at : at + LANES], pots[:, at : at + LANES]) for at in range(0, even, LANES)]
-    end = merged(tiles[:, :, even:])
+    end = tiles[:, even:]
     volume = gram(jnp.concatenate(parts, axis=1), tile) + gram(weighted(end, pots[:, even:]), end)
 
     def add_comp(comp, kinetic):
         grad_move(comp).wait()
-        slope = merged(grads[comp, :, :, :even])
-        end = merged(grads[comp, :, :, even:])
+        slope = grads[comp, :, :even]
+        end = grads[comp, :, even:]
         return kinetic + gram(slope, slope) + gram(end, end)
 
     kinetic = lax.fori_loop(0, comps, add_comp, jnp.zeros((rows, rows), jnp.float32))
@@ -139,7 +139,11 @@
     for element, pair in enumerate(pairs):
         rows[pl.ds(2 * element, width, stride=kinds), :] = diag[element]
         rows[pl.ds(2 * element + 1, width, stride=kinds), :] = pair
-    for slot, owner in enumerate(exchange_order(out.shape[0])):
+    ways = out.shape[0] // 2
+    start = own_slots(ways)
+    slots = [exchange_order(ways).index(owner) for owner in range(ways)]
+    out[pl.ds(ways - start, ways)] = jnp.zeros((ways, kinds, share), jnp.float32)
+    for owner in range(ways):
         at, end = owner * share, (owner + 1) * share
         pieces = []
         while at < end:
@@ -147,15 +151,36 @@
             size = min(width - col, end - at)
             pieces.append(rows[pl.ds(kinds * row, kinds), pl.ds(col, size)])
             at += size
-        out[slot] = jnp.concatenate(pieces, axis=1)
+        out[start + slots[owner]] = jnp.concatenate(pieces, axis=1)
+
+
+def own_slots(ways):
+    return ways * (lax.rem(lax.axis_index("elem") // 2, 4) // 2)
 
 
 def exchange_order(ways):
-    return [(slot + ways * 11 // 16) % ways for slot in range(ways)]
+    rings = max(ways // 2, 1)
+    root = 2 * (5 * rings // 8) + 1 if ways > 1 else 0
+
+    def hops(share):
+        step = (share // 2 - root // 2) % rings
+        return min(step, rings - step) + 4 * ((share ^ root) & 1)
+
+    return [root] + sorted((share for share in range(ways) if share != root), key=hops, reverse=True)
+
+
+def exchange_groups(elems, ways):
+    order = exchange_order(ways)
+    return [
+        [row * ways + share for row in (elem, elem + 4) for share in order]
+        for elem in range(elems)
+        if (elem // 2) % 4 < 2
+    ]
 
 
 def total_terms(shared, out):
-    total = jnp.sum(shared[...], axis=0)
+    ways = shared.shape[0] // 2
+    total = jnp.sum(shared[pl.ds(own_slots(ways), ways)], axis=0)
     for element in range(out.shape[0]):
         out[element] = total[2 * element : 2 * element + 2]
 
@@ -191,10 +216,10 @@
         in_specs=[any_space] * 6,
         out_specs=[in_vmem] * 4,
         scratch_shapes=[
-            pltpu.VMEM(grad.shape, jnp.bfloat16),
-            pltpu.VMEM(vals.shape, jnp.bfloat16),
+            pltpu.VMEM((comps, rows, points), jnp.bfloat16),
+            pltpu.VMEM((rows, points), jnp.bfloat16),
             pltpu.VMEM(potential.shape, jnp.float32),
-            pltpu.VMEM(faces.shape, jnp.bfloat16),
+            pltpu.VMEM((count, 2, rows, face_points), jnp.bfloat16),
             pltpu.SMEM(penalty.shape, jnp.float32),
             pltpu.SMEM(orientation.shape, jnp.int32),
             *fold_scratch,
@@ -208,14 +233,15 @@
     share = width * width // ways
     terms = pl.pallas_call(
         pair_terms,
-        out_shape=pltpu.VMEM((ways, 2 * count, share), jnp.float32),
+        out_shape=pltpu.VMEM((2 * ways, 2 * count, share), jnp.float32),
         in_specs=[in_vmem] * 5,
         out_specs=in_vmem,
         scratch_shapes=[*fold_scratch, pltpu.VMEM((2 * count * width, width), jnp.float32)],
         compiler_params=pltpu.CompilerParams(vmem_limit_bytes=8 * MIB),
         name="pair_terms",
     )(pltpu.with_memory_space_constraint(arrived, pltpu.VMEM), edge, cross, scales, diag)
-    shared = lax.all_to_all(terms, "basis", 0, 0, axis_index_groups=[exchange_order(ways)])
+    groups = exchange_groups(lax.axis_size("elem"), ways)
+    shared = lax.all_to_all(terms, ("elem", "basis"), 0, 0, axis_index_groups=groups)
     return pl.pallas_call(
         total_terms,
         out_shape=jax.ShapeDtypeStruct((count, 2, share), jnp.float32),

time: 33.4 us -> 33 us (0.988)
  the two profiles are of different devices: /device:TPU:63 before, /device:TPU:16 now
where the time goes in v3:
time: 33 us; the launch traced here: 32.8 us
  blocking collectives  26.6 us (81%)
  Pallas kernels  4.23 us (13%)
  starting transfers between devices  1.91 us (6%)
    all_to_all x1, blocking collectives, on_device(): lax.all_to_all(terms, ('elem', 'basis'), 0, 0, axis_index_groups=groups)  26.6 us
    pallas_call x1, Pallas kernels, on_device(): pl.pallas_call(local_terms, out_shape=[pltpu.VMEM((count, width, width),...  3.15 us
    ppermute x1, starting transfers between devices, from_behind(): return lax.ppermute(value, axis, pairs)  1.91 us
  transfers between devices with their start and end apart: 1, of which 0 were waited for; matrix products, arithmetic and copies ran while one was open for 0% of the time, Pallas kernels for 10%

profile of v3, /device:TPU:16, one launch (start us, length us, event | category | flops | bytes accessed | tf_op | source)
XLA Modules:
  0.0 32.8 jit_solution(17671755343786415235)
XLA Ops:
  0.0 1.9 %collective-permute-start = (bf16[2,2,60,2,81]{4,3,2,1,0:T(2,128)(2,1)}, bf16[2,2,60,2,81]{4,3,2,1,0:T(2,128)(2,1)S(1)}, u32[]{:S(2)}, u32[]{:S(2)}) collective-permute-start(bf16[2,2,60,2,81]{4,3,2,1,0:T(2,128)(2,1)} %bitcast.5), channel_id=1, source_target_pairs={{0,496},{16,0},{32,16},{48,32},{64,48},{80,64},{96,80},{112,96},{1... | collective-permute-start | bytes 233288 | tf_op jit(solution)/shard_map/ppermute | solution.py:191
  1.9 3.1 %local_terms.1 = (f32[2,60,60]{2,1,0:T(8,128)S(1)}, f32[120,120]{1,0:T(8,128)S(1)}, f32[2,120,120]{2,1,0:T(8,128)S(1)}, bf16[120,81]{1,0:T(8,128)(2,1)S(1)}) custom-call(bf16[3,60,2,2916]{3,2,1,0:T(2,128)(2,1)} %bitcast.3, bf16[60,2,2916]{2,1,0:T(2,128)(2,1)} %bitcast.4, f32[2,2916]{1,0:T(2,128)} %pot.1, bf16[2,2,60,2,81]{4,3,2,1,0:T(2,128)(2,1)} %bitcast.6, ...), custom_call_target="tpu_custom_call" | custom-call | flops 400000000 | bytes 3000000 | tf_op jit(solution)/shard_map/local_terms/pallas_call | solution.py:208
  5.1 0.0 collective-permute-done.arrived
  5.1 0.5 %pair_terms.1 = f32[32,4,225]{2,1,0:T(4,128)S(1)} custom-call(bf16[2,2,60,2,81]{4,3,2,1,0:T(2,128)(2,1)S(1)} %collective-permute-done.arrived, bf16[120,81]{1,0:T(8,128)(2,1)S(1)} %get-tuple-element.9.edge, f32[120,120]{1,0:T(8,128)S(1)} %get-tuple-element.10.cross, f32[2,120,120]{2,1,0:T(8,128)S(1)} %get-tuple-element.11.scales, ...), custom_call_target="tpu_custom_call" | custom-call | tf_op jit(solution)/shard_map/pair_terms/pallas_call | solution.py:234
  5.6 26.6 %all_to_all.5.shared = f32[32,4,225]{2,1,0:T(4,128)S(1)} all-to-all(f32[32,4,225]{2,1,0:T(4,128)S(1)} %pair_terms.1), channel_id=1, replica_groups={{11,2,0,4,6,14,8,12,3,10,1,5,7,15,9,13,75,66,64,68,70,78,72,76,67,74,65..., dimensions={0} | all-to-all | bytes 230400 | tf_op jit(solution)/shard_map/all_to_all | solution.py:244
  32.2 0.6 %total_terms.1 = f32[2,2,225]{2,1,0:T(2,128)} custom-call(f32[32,4,225]{2,1,0:T(4,128)S(1)} %all_to_all.5.shared), custom_call_target="tpu_custom_call" | custom-call | tf_op jit(solution)/shard_map/total_terms/pallas_call | solution.py:245
Async XLA Ops:
  0.0 5.1 %collective-permute-start = (bf16[2,2,60,2,81]{4,3,2,1,0:T(2,128)(2,1)}, bf16[2,2,60,2,81]{4,3,2,1,0:T(2,128)(2,1)S(1)}, u32[]{:S(2)}, u32[]{:S(2)}) collective-permute-start(bf16[2,2,60,2,81]{4,3,2,1,0:T(2,128)(2,1)} %bitcast.5), channel_id=1, source_target_pairs={{0,496},{16,0},{32,16},{48,32},{64,48},{80,64},{96,80},{112,96},{1... | collective-permute-start | bytes 233288 | tf_op jit(solution)/shard_map/ppermute | solution.py:191

commit v4 on v3

--- a/solution.py
+++ b/solution.py
@@ -115,6 +115,10 @@
     end = tiles[:, even:]
     volume = gram(jnp.concatenate(parts, axis=1), tile) + gram(weighted(end, pots[:, even:]), end)
 
+    masks = [(row == element) & (col == element) for element in range(count)]
+    inner = 0.5 * (volume + volume.T)
+    steady = [jnp.where(mask, inner, 0.0) + part for mask, part in zip(masks, face_parts)]
+
     def add_comp(comp, kinetic):
         grad_move(comp).wait()
         slope = grads[comp, :, :even]
@@ -122,10 +126,7 @@
         return kinetic + gram(slope, slope) + gram(end, end)
 
     kinetic = lax.fori_loop(0, comps, add_comp, jnp.zeros((rows, rows), jnp.float32))
-    inner = 0.5 * (volume + volume.T) + (0.5 / PTS) * kinetic
-    parts = [
-        jnp.where((row == element) & (col == element), inner, 0.0) + face_parts[element] for element in range(count)
-    ]
+    parts = [part + jnp.where(mask, (0.5 / PTS) * kinetic, 0.0) for part, mask in zip(steady, masks)]
     diag[0], diag[1] = fold(*parts, stage, turned, width)
 
 
@@ -155,7 +156,9 @@
 
 
 def own_slots(ways):
-    return ways * (lax.rem(lax.axis_index("elem") // 2, 4) // 2)
+    elem = lax.axis_index("elem")
+    second = lax.rem(elem // 2, 4) // 2
+    return ways * jnp.where((elem == 0) | (elem == 4), 1 - second, second)
 
 
 def exchange_order(ways):
@@ -172,7 +175,7 @@
 def exchange_groups(elems, ways):
     order = exchange_order(ways)
     return [
-        [row * ways + share for row in (elem, elem + 4) for share in order]
+        [row * ways + share for row in ((elem, elem + 4) if elem else (4, 0)) for share in order]
         for elem in range(elems)
         if (elem // 2) % 4 < 2
     ]

time: 33 us -> 32.3 us (0.979)
  the two profiles are of different devices: /device:TPU:16 before, /device:TPU:15 now
where the time goes in v4:
time: 32.3 us; the launch traced here: 32.1 us
  blocking collectives  24.5 us (76%)
  Pallas kernels  4.26 us (13%)
  starting transfers between devices  2.57 us (8%)
  waiting for transfers between devices  0.76 us (2%)
    all_to_all x1, blocking collectives, on_device(): lax.all_to_all(terms, ('elem', 'basis'), 0, 0, axis_index_groups=groups)  24.5 us
    pallas_call x1, Pallas kernels, on_device(): pl.pallas_call(local_terms, out_shape=[pltpu.VMEM((count, width, width),...  3.17 us
    ppermute x1, starting transfers between devices, from_behind(): return lax.ppermute(value, axis, pairs)  2.57 us
    ppermute x1, waiting for transfers between devices, from_behind(): return lax.ppermute(value, axis, pairs)  0.76 us
  transfers between devices with their start and end apart: 1, of which 1 were waited for; matrix products, arithmetic and copies ran while one was open for 0% of the time, Pallas kernels for 10%

profile of v4, /device:TPU:15, one launch (start us, length us, event | category | flops | bytes accessed | tf_op | source)
XLA Modules:
  0.0 32.1 jit_solution(8231972136383833366)
XLA Ops:
  0.0 2.6 %collective-permute-start = (bf16[2,2,60,2,81]{4,3,2,1,0:T(2,128)(2,1)}, bf16[2,2,60,2,81]{4,3,2,1,0:T(2,128)(2,1)S(1)}, u32[]{:S(2)}, u32[]{:S(2)}) collective-permute-start(bf16[2,2,60,2,81]{4,3,2,1,0:T(2,128)(2,1)} %bitcast.5), channel_id=1, source_target_pairs={{0,496},{16,0},{32,16},{48,32},{64,48},{80,64},{96,80},{112,96},{1... | collective-permute-start | bytes 233288 | tf_op jit(solution)/shard_map/ppermute | solution.py:194
  2.6 3.2 %local_terms.1 = (f32[2,60,60]{2,1,0:T(8,128)S(1)}, f32[120,120]{1,0:T(8,128)S(1)}, f32[2,120,120]{2,1,0:T(8,128)S(1)}, bf16[120,81]{1,0:T(8,128)(2,1)S(1)}) custom-call(bf16[3,60,2,2916]{3,2,1,0:T(2,128)(2,1)} %bitcast.3, bf16[60,2,2916]{2,1,0:T(2,128)(2,1)} %bitcast.4, f32[2,2916]{1,0:T(2,128)} %pot.1, bf16[2,2,60,2,81]{4,3,2,1,0:T(2,128)(2,1)} %bitcast.6, ...), custom_call_target="tpu_custom_call" | custom-call | flops 400000000 | bytes 3000000 | tf_op jit(solution)/shard_map/local_terms/pallas_call | solution.py:211
  5.8 0.8 %collective-permute-done.arrived = bf16[2,2,60,2,81]{4,3,2,1,0:T(2,128)(2,1)S(1)} collective-permute-done((bf16[2,2,60,2,81]{4,3,2,1,0:T(2,128)(2,1)}, bf16[2,2,60,2,81]{4,3,2,1,0:T(2,128)(2,1)S(1)}, u32[]{:S(2)}, u32[]{:S(2)}) %collective-permute-start) | collective-permute-done | bytes 77792 | tf_op jit(solution)/shard_map/ppermute | solution.py:194
  6.5 0.5 %pair_terms.1 = f32[32,4,225]{2,1,0:T(4,128)S(1)} custom-call(bf16[2,2,60,2,81]{4,3,2,1,0:T(2,128)(2,1)S(1)} %collective-permute-done.arrived, bf16[120,81]{1,0:T(8,128)(2,1)S(1)} %get-tuple-element.9.edge, f32[120,120]{1,0:T(8,128)S(1)} %get-tuple-element.10.cross, f32[2,120,120]{2,1,0:T(8,128)S(1)} %get-tuple-element.11.scales, ...), custom_call_target="tpu_custom_call" | custom-call | tf_op jit(solution)/shard_map/pair_terms/pallas_call | solution.py:237
  7.0 24.5 %all_to_all.5.shared = f32[32,4,225]{2,1,0:T(4,128)S(1)} all-to-all(f32[32,4,225]{2,1,0:T(4,128)S(1)} %pair_terms.1), channel_id=1, replica_groups={{75,66,64,68,70,78,72,76,67,74,65,69,71,79,73,77,11,2,0,4,6,14,8,12,3,1..., dimensions={0} | all-to-all | bytes 230400 | tf_op jit(solution)/shard_map/all_to_all | solution.py:247
  31.5 0.6 %total_terms.1 = f32[2,2,225]{2,1,0:T(2,128)} custom-call(f32[32,4,225]{2,1,0:T(4,128)S(1)} %all_to_all.5.shared), custom_call_target="tpu_custom_call" | custom-call | tf_op jit(solution)/shard_map/total_terms/pallas_call | solution.py:248
Async XLA Ops:
  0.0 6.5 %collective-permute-start = (bf16[2,2,60,2,81]{4,3,2,1,0:T(2,128)(2,1)}, bf16[2,2,60,2,81]{4,3,2,1,0:T(2,128)(2,1)S(1)}, u32[]{:S(2)}, u32[]{:S(2)}) collective-permute-start(bf16[2,2,60,2,81]{4,3,2,1,0:T(2,128)(2,1)} %bitcast.5), channel_id=1, source_target_pairs={{0,496},{16,0},{32,16},{48,32},{64,48},{80,64},{96,80},{112,96},{1... | collective-permute-start | bytes 233288 | tf_op jit(solution)/shard_map/ppermute | solution.py:194

commit v5 on v4

--- a/solution.py
+++ b/solution.py
@@ -1,3 +1,5 @@
+import math
+
 import jax
 import jax.numpy as jnp
 from jax import lax
@@ -28,19 +30,21 @@
     return row, col
 
 
-def fold(first, second, stage, turned, width):
-    size = first.shape[0]
+def fold(matrices, stage, turned, width):
+    size = matrices[0].shape[0]
     half = size // 2
-    stage[0] = first
-    stage[1] = second
-    rows = [stage[n, pl.ds(0, half, stride=2), :] + stage[n, pl.ds(1, half, stride=2), :] for n in range(2)]
-    turned[...] = jnp.concatenate(rows, axis=0).T
-    both = turned[pl.ds(0, half, stride=2), :] + turned[pl.ds(1, half, stride=2), :]
-    return both[:width, :width], both[:width, half : half + width]
-
-
-def local_terms(grad, vals, pot, faces, penalty, orientation, diag, cross, scales, edge, grads, tiles, pots, sides,
-                pens, codes, stage, turned, sems):
+    rows = []
+    for n, matrix in enumerate(matrices):
+        stage[n] = matrix
+        rows.append(stage[n, pl.ds(0, half, stride=2), :] + stage[n, pl.ds(1, half, stride=2), :])
+    wide = half * len(rows)
+    turned[:, :wide] = jnp.concatenate(rows, axis=0).T
+    both = turned[pl.ds(0, half, stride=2), :wide] + turned[pl.ds(1, half, stride=2), :wide]
+    return [both[:width, n * half : n * half + width] for n in range(len(rows))]
+
+
+def local_terms(grad, vals, pot, faces, penalty, orientation, chunks, scales, edge, grads, tiles, pots, sides,
+                pens, codes, stage, turned, blocks, sems):
     comps, width, count, points = grad.shape
     even = points // LANES * LANES
     rows = width * count
@@ -95,7 +99,10 @@
             jnp.where(col == 0, -0.25 * lower_sign, 0.0),
         )
 
-    cross[...] = cross_scale(0) * gram(lowers[1], uppers[0])
+    (pair,) = fold([cross_scale(0) * gram(lowers[1], uppers[0])], stage, turned, width)
+    kinds = 2 * count
+    blocks[pl.ds(1, width, stride=kinds), :] = pair
+    blocks[pl.ds(kinds - 1, width, stride=kinds), :] = jnp.zeros((width, width), jnp.float32)
     edge[...] = uppers[count - 1]
     scale = cross_scale(count - 1)
     for side in range(2):
@@ -127,32 +134,52 @@
 
     kinetic = lax.fori_loop(0, comps, add_comp, jnp.zeros((rows, rows), jnp.float32))
     parts = [part + jnp.where(mask, (0.5 / PTS) * kinetic, 0.0) for part, mask in zip(steady, masks)]
-    diag[0], diag[1] = fold(*parts, stage, turned, width)
-
-
-def pair_terms(arrived, edge, cross, scales, diag, out, stage, turned, rows):
-    width = diag.shape[1]
-    share = out.shape[2]
+    for element, diag in enumerate(fold(parts, stage, turned, width)):
+        blocks[pl.ds(2 * element, width, stride=kinds), :] = diag
+
+    share = chunks.shape[2]
+    ways = chunks.shape[0] // 2
+    start = own_slots(ways)
+    chunks[pl.ds(ways - start, ways)] = jnp.zeros((ways, kinds, share), jnp.float32)
+    for slot, owner in enumerate(exchange_order(ways)):
+        pieces = [
+            blocks[pl.ds(kinds * row, kinds), pl.ds(col, size)]
+            for row, col, size in spans_of(owner * share, share, width)
+        ]
+        chunks[start + slot] = jnp.concatenate(pieces, axis=1)
+
+
+def spans_of(at, share, width):
+    end = at + share
+    while at < end:
+        row, col = divmod(at, width)
+        size = min(width - col, end - at)
+        yield row, col, size
+        at += size
+
+
+def pair_terms(arrived, edge, scales, chunks, out, stage, turned, rows):
+    kinds, share = chunks.shape[1:]
+    ways = chunks.shape[0] // 2
+    width = rows.shape[0]
     upper = edge[...]
     parts = [gram(merged(arrived[0, side]), upper) * scales[side] for side in range(2)]
-    pairs = fold(cross[...], parts[0] + parts[1], stage, turned, width)
-    kinds = 2 * len(pairs)
-    for element, pair in enumerate(pairs):
-        rows[pl.ds(2 * element, width, stride=kinds), :] = diag[element]
-        rows[pl.ds(2 * element + 1, width, stride=kinds), :] = pair
-    ways = out.shape[0] // 2
+    (rows[...],) = fold([parts[0] + parts[1]], stage, turned, width)
     start = own_slots(ways)
-    slots = [exchange_order(ways).index(owner) for owner in range(ways)]
-    out[pl.ds(ways - start, ways)] = jnp.zeros((ways, kinds, share), jnp.float32)
-    for owner in range(ways):
-        at, end = owner * share, (owner + 1) * share
-        pieces = []
-        while at < end:
-            row, col = divmod(at, width)
-            size = min(width - col, end - at)
-            pieces.append(rows[pl.ds(kinds * row, kinds), pl.ds(col, size)])
-            at += size
-        out[start + slots[owner]] = jnp.concatenate(pieces, axis=1)
+    out[pl.ds(ways - start, ways)] = chunks[pl.ds(ways - start, ways)]
+    order = exchange_order(ways)
+    last = lax.broadcasted_iota(jnp.int32, (kinds, share), 0) == kinds - 1
+    groups = math.gcd(ways, width)
+    stride = width // groups
+    for step in range(ways // groups):
+        pieces = [
+            rows[pl.ds(row, groups, stride=stride), :][:, col : col + size]
+            for row, col, size in spans_of(step * share, share, width)
+        ]
+        added = jnp.concatenate(pieces, axis=1)
+        for group in range(groups):
+            slot = start + order.index(group * (ways // groups) + step)
+            out[slot] = jnp.where(last, added[group : group + 1], chunks[slot])
 
 
 def own_slots(ways):
@@ -208,16 +235,18 @@
     any_space = pl.BlockSpec(memory_space=pl.ANY)
     in_vmem = pl.BlockSpec(memory_space=pltpu.VMEM)
     fold_scratch = [pltpu.VMEM((2, rows, rows), jnp.float32), pltpu.VMEM((rows, rows), jnp.float32)]
-    diag, cross, scales, edge = pl.pallas_call(
+    ways = lax.axis_size("basis")
+    share = width * width // ways
+    terms = pltpu.VMEM((2 * ways, 2 * count, share), jnp.float32)
+    chunks, scales, edge = pl.pallas_call(
         local_terms,
         out_shape=[
-            pltpu.VMEM((count, width, width), jnp.float32),
-            pltpu.VMEM((rows, rows), jnp.float32),
+            terms,
             pltpu.VMEM((2, rows, rows), jnp.float32),
             pltpu.VMEM((rows, face_points), jnp.bfloat16),
         ],
         in_specs=[any_space] * 6,
-        out_specs=[in_vmem] * 4,
+        out_specs=[in_vmem] * 3,
         scratch_shapes=[
             pltpu.VMEM((comps, rows, points), jnp.bfloat16),
             pltpu.VMEM((rows, points), jnp.bfloat16),
@@ -226,23 +255,22 @@
             pltpu.SMEM(penalty.shape, jnp.float32),
             pltpu.SMEM(orientation.shape, jnp.int32),
             *fold_scratch,
+            pltpu.VMEM((2 * count * width, width), jnp.float32),
             pltpu.SemaphoreType.DMA((comps + 5,)),
         ],
         compiler_params=pltpu.CompilerParams(vmem_limit_bytes=16 * MIB),
         cost_estimate=pl.CostEstimate(flops=400_000_000, bytes_accessed=3_000_000, transcendentals=0),
         name="local_terms",
     )(*held)
-    ways = lax.axis_size("basis")
-    share = width * width // ways
     terms = pl.pallas_call(
         pair_terms,
-        out_shape=pltpu.VMEM((2 * ways, 2 * count, share), jnp.float32),
-        in_specs=[in_vmem] * 5,
+        out_shape=terms,
+        in_specs=[in_vmem] * 4,
         out_specs=in_vmem,
-        scratch_shapes=[*fold_scratch, pltpu.VMEM((2 * count * width, width), jnp.float32)],
+        scratch_shapes=[*fold_scratch, pltpu.VMEM((width, width), jnp.float32)],
         compiler_params=pltpu.CompilerParams(vmem_limit_bytes=8 * MIB),
         name="pair_terms",
-    )(pltpu.with_memory_space_constraint(arrived, pltpu.VMEM), edge, cross, scales, diag)
+    )(pltpu.with_memory_space_constraint(arrived, pltpu.VMEM), edge, scales, chunks)
     groups = exchange_groups(lax.axis_size("elem"), ways)
     shared = lax.all_to_all(terms, ("elem", "basis"), 0, 0, axis_index_groups=groups)
     return pl.pallas_call(

time: 32.3 us -> 32.2 us (level)
  no operation moved by 1% of the time
where the time goes in v5:
time: 32.2 us; the launch traced here: 32 us
  blocking collectives  24.5 us (76%)
  Pallas kernels  4.29 us (13%)
  starting transfers between devices  2.57 us (8%)
  waiting for transfers between devices  0.64 us (2%)
    all_to_all x1, blocking collectives, on_device(): lax.all_to_all(terms, ('elem', 'basis'), 0, 0, axis_index_groups=groups)  24.5 us
    pallas_call x1, Pallas kernels, on_device(): pl.pallas_call(local_terms, out_shape=[terms, pltpu.VMEM((2, rows, rows),...  3.29 us
    ppermute x1, starting transfers between devices, from_behind(): return lax.ppermute(value, axis, pairs)  2.57 us
  transfers between devices with their start and end apart: 1, of which 1 were waited for; matrix products, arithmetic and copies ran while one was open for 0% of the time, Pallas kernels for 10%

profile of v5, /device:TPU:15, one launch (start us, length us, event | category | flops | bytes accessed | tf_op | source)
XLA Modules:
  0.0 32.0 jit_solution(561844636387809468)
XLA Ops:
  0.0 2.6 %collective-permute-start = (bf16[2,2,60,2,81]{4,3,2,1,0:T(2,128)(2,1)}, bf16[2,2,60,2,81]{4,3,2,1,0:T(2,128)(2,1)S(1)}, u32[]{:S(2)}, u32[]{:S(2)}) collective-permute-start(bf16[2,2,60,2,81]{4,3,2,1,0:T(2,128)(2,1)} %bitcast.5), channel_id=1, source_target_pairs={{0,496},{16,0},{32,16},{48,32},{64,48},{80,64},{96,80},{112,96},{1... | collective-permute-start | bytes 233288 | tf_op jit(solution)/shard_map/ppermute | solution.py:221
  2.6 3.3 %local_terms.1 = (f32[32,4,225]{2,1,0:T(4,128)S(1)}, f32[2,120,120]{2,1,0:T(8,128)S(1)}, bf16[120,81]{1,0:T(8,128)(2,1)S(1)}) custom-call(bf16[3,60,2,2916]{3,2,1,0:T(2,128)(2,1)} %bitcast.3, bf16[60,2,2916]{2,1,0:T(2,128)(2,1)} %bitcast.4, f32[2,2916]{1,0:T(2,128)} %pot.1, bf16[2,2,60,2,81]{4,3,2,1,0:T(2,128)(2,1)} %bitcast.6, f32[64]{0:T(128)} %penalty.1, ...), custom_call_target="tpu_custom_call" | custom-call | flops 400000000 | bytes 3000000 | tf_op jit(solution)/shard_map/local_terms/pallas_call | solution.py:241
  5.9 0.6 %collective-permute-done.arrived = bf16[2,2,60,2,81]{4,3,2,1,0:T(2,128)(2,1)S(1)} collective-permute-done((bf16[2,2,60,2,81]{4,3,2,1,0:T(2,128)(2,1)}, bf16[2,2,60,2,81]{4,3,2,1,0:T(2,128)(2,1)S(1)}, u32[]{:S(2)}, u32[]{:S(2)}) %collective-permute-start) | collective-permute-done | bytes 77792 | tf_op jit(solution)/shard_map/ppermute | solution.py:221
  6.5 0.4 %pair_terms.1 = f32[32,4,225]{2,1,0:T(4,128)S(1)} custom-call(bf16[2,2,60,2,81]{4,3,2,1,0:T(2,128)(2,1)S(1)} %collective-permute-done.arrived, bf16[120,81]{1,0:T(8,128)(2,1)S(1)} %get-tuple-element.8.edge, f32[2,120,120]{2,1,0:T(8,128)S(1)} %get-tuple-element.9.scales, f32[32,4,225]{2,1,0:T(4,128)S(1)} %get-tuple-element.10.chunks), custom_call_target="tpu_custom_call" | custom-call | tf_op jit(solution)/shard_map/pair_terms/pallas_call | solution.py:265
  6.9 24.5 %all_to_all.5.shared = f32[32,4,225]{2,1,0:T(4,128)S(1)} all-to-all(f32[32,4,225]{2,1,0:T(4,128)S(1)} %pair_terms.1), channel_id=1, replica_groups={{75,66,64,68,70,78,72,76,67,74,65,69,71,79,73,77,11,2,0,4,6,14,8,12,3,1..., dimensions={0} | all-to-all | bytes 230400 | tf_op jit(solution)/shard_map/all_to_all | solution.py:275
  31.4 0.6 %total_terms.1 = f32[2,2,225]{2,1,0:T(2,128)} custom-call(f32[32,4,225]{2,1,0:T(4,128)S(1)} %all_to_all.5.shared), custom_call_target="tpu_custom_call" | custom-call | tf_op jit(solution)/shard_map/total_terms/pallas_call | solution.py:276
Async XLA Ops:
  0.0 6.5 %collective-permute-start = (bf16[2,2,60,2,81]{4,3,2,1,0:T(2,128)(2,1)}, bf16[2,2,60,2,81]{4,3,2,1,0:T(2,128)(2,1)S(1)}, u32[]{:S(2)}, u32[]{:S(2)}) collective-permute-start(bf16[2,2,60,2,81]{4,3,2,1,0:T(2,128)(2,1)} %bitcast.5), channel_id=1, source_target_pairs={{0,496},{16,0},{32,16},{48,32},{64,48},{80,64},{96,80},{112,96},{1... | collective-permute-start | bytes 233288 | tf_op jit(solution)/shard_map/ppermute | solution.py:221

commit v6 on v5

--- a/solution.py
+++ b/solution.py
@@ -190,7 +190,7 @@
 
 def exchange_order(ways):
     rings = max(ways // 2, 1)
-    root = 2 * (5 * rings // 8) + 1 if ways > 1 else 0
+    root = 2 * (rings // 2) + 1 if ways > 1 else 0
 
     def hops(share):
         step = (share // 2 - root // 2) % rings

time: 32.2 us -> 32.5 us (level)
  the two profiles are of different devices: /device:TPU:15 before, /device:TPU:48 now
where the time goes in v6:
time: 32.5 us; the launch traced here: 32.4 us
  blocking collectives  25.3 us (78%)
  Pallas kernels  4.34 us (13%)
  starting transfers between devices  2.68 us (8%)
    all_to_all x1, blocking collectives, on_device(): lax.all_to_all(terms, ('elem', 'basis'), 0, 0, axis_index_groups=groups)  25.3 us
    pallas_call x1, Pallas kernels, on_device(): pl.pallas_call(local_terms, out_shape=[terms, pltpu.VMEM((2, rows, rows),...  3.35 us
    ppermute x1, starting transfers between devices, from_behind(): return lax.ppermute(value, axis, pairs)  2.68 us
  transfers between devices with their start and end apart: 1, of which 0 were waited for; matrix products, arithmetic and copies ran while one was open for 0% of the time, Pallas kernels for 10%

profile of v6, /device:TPU:48, one launch (start us, length us, event | category | flops | bytes accessed | tf_op | source)
XLA Modules:
  0.0 32.4 jit_solution(18183849946261647167)
XLA Ops:
  0.0 2.7 %collective-permute-start = (bf16[2,2,60,2,81]{4,3,2,1,0:T(2,128)(2,1)}, bf16[2,2,60,2,81]{4,3,2,1,0:T(2,128)(2,1)S(1)}, u32[]{:S(2)}, u32[]{:S(2)}) collective-permute-start(bf16[2,2,60,2,81]{4,3,2,1,0:T(2,128)(2,1)} %bitcast.5), channel_id=1, source_target_pairs={{0,496},{16,0},{32,16},{48,32},{64,48},{80,64},{96,80},{112,96},{1... | collective-permute-start | bytes 233288 | tf_op jit(solution)/shard_map/ppermute | solution.py:221
  2.7 3.3 %local_terms.1 = (f32[32,4,225]{2,1,0:T(4,128)S(1)}, f32[2,120,120]{2,1,0:T(8,128)S(1)}, bf16[120,81]{1,0:T(8,128)(2,1)S(1)}) custom-call(bf16[3,60,2,2916]{3,2,1,0:T(2,128)(2,1)} %bitcast.3, bf16[60,2,2916]{2,1,0:T(2,128)(2,1)} %bitcast.4, f32[2,2916]{1,0:T(2,128)} %pot.1, bf16[2,2,60,2,81]{4,3,2,1,0:T(2,128)(2,1)} %bitcast.6, f32[64]{0:T(128)} %penalty.1, ...), custom_call_target="tpu_custom_call" | custom-call | flops 400000000 | bytes 3000000 | tf_op jit(solution)/shard_map/local_terms/pallas_call | solution.py:241
  6.0 0.0 collective-permute-done.arrived
  6.1 0.4 %pair_terms.1 = f32[32,4,225]{2,1,0:T(4,128)S(1)} custom-call(bf16[2,2,60,2,81]{4,3,2,1,0:T(2,128)(2,1)S(1)} %collective-permute-done.arrived, bf16[120,81]{1,0:T(8,128)(2,1)S(1)} %get-tuple-element.8.edge, f32[2,120,120]{2,1,0:T(8,128)S(1)} %get-tuple-element.9.scales, f32[32,4,225]{2,1,0:T(4,128)S(1)} %get-tuple-element.10.chunks), custom_call_target="tpu_custom_call" | custom-call | tf_op jit(solution)/shard_map/pair_terms/pallas_call | solution.py:265
  6.4 25.3 %all_to_all.5.shared = f32[32,4,225]{2,1,0:T(4,128)S(1)} all-to-all(f32[32,4,225]{2,1,0:T(4,128)S(1)} %pair_terms.1), channel_id=1, replica_groups={{73,64,66,78,68,76,70,74,65,72,67,79,69,77,71,75,9,0,2,14,4,12,6,10,1,8..., dimensions={0} | all-to-all | bytes 230400 | tf_op jit(solution)/shard_map/all_to_all | solution.py:275
  31.7 0.6 %total_terms.1 = f32[2,2,225]{2,1,0:T(2,128)} custom-call(f32[32,4,225]{2,1,0:T(4,128)S(1)} %all_to_all.5.shared), custom_call_target="tpu_custom_call" | custom-call | tf_op jit(solution)/shard_map/total_terms/pallas_call | solution.py:276
Async XLA Ops:
  0.0 6.0 %collective-permute-start = (bf16[2,2,60,2,81]{4,3,2,1,0:T(2,128)(2,1)}, bf16[2,2,60,2,81]{4,3,2,1,0:T(2,128)(2,1)S(1)}, u32[]{:S(2)}, u32[]{:S(2)}) collective-permute-start(bf16[2,2,60,2,81]{4,3,2,1,0:T(2,128)(2,1)} %bitcast.5), channel_id=1, source_target_pairs={{0,496},{16,0},{32,16},{48,32},{64,48},{80,64},{96,80},{112,96},{1... | collective-permute-start | bytes 233288 | tf_op jit(solution)/shard_map/ppermute | solution.py:221

commit v7 on v5

--- a/solution.py
+++ b/solution.py
@@ -132,7 +132,9 @@
         end = grads[comp, :, even:]
         return kinetic + gram(slope, slope) + gram(end, end)
 
-    kinetic = lax.fori_loop(0, comps, add_comp, jnp.zeros((rows, rows), jnp.float32))
+    kinetic = jnp.zeros((rows, rows), jnp.float32)
+    for comp in range(comps):
+        kinetic = add_comp(comp, kinetic)
     parts = [part + jnp.where(mask, (0.5 / PTS) * kinetic, 0.0) for part, mask in zip(steady, masks)]
     for element, diag in enumerate(fold(parts, stage, turned, width)):
         blocks[pl.ds(2 * element, width, stride=kinds), :] = diag

time: 32.2 us -> 32.5 us (level)
  the two profiles are of different devices: /device:TPU:15 before, /device:TPU:48 now
where the time goes in v7:
time: 32.5 us; the launch traced here: 32.3 us
  blocking collectives  24.8 us (76%)
  Pallas kernels  4.81 us (15%)
  starting transfers between devices  2.68 us (8%)
    all_to_all x1, blocking collectives, on_device(): lax.all_to_all(terms, ('elem', 'basis'), 0, 0, axis_index_groups=groups)  24.8 us
    pallas_call x1, Pallas kernels, on_device(): pl.pallas_call(local_terms, out_shape=[terms, pltpu.VMEM((2, rows, rows),...  3.82 us
    ppermute x1, starting transfers between devices, from_behind(): return lax.ppermute(value, axis, pairs)  2.68 us
  transfers between devices with their start and end apart: 1, of which 0 were waited for; matrix products, arithmetic and copies ran while one was open for 0% of the time, Pallas kernels for 12%

profile of v7, /device:TPU:48, one launch (start us, length us, event | category | flops | bytes accessed | tf_op | source)
XLA Modules:
  0.0 32.3 jit_solution(16884769606268031508)
XLA Ops:
  0.0 2.7 %collective-permute-start = (bf16[2,2,60,2,81]{4,3,2,1,0:T(2,128)(2,1)}, bf16[2,2,60,2,81]{4,3,2,1,0:T(2,128)(2,1)S(1)}, u32[]{:S(2)}, u32[]{:S(2)}) collective-permute-start(bf16[2,2,60,2,81]{4,3,2,1,0:T(2,128)(2,1)} %bitcast.5), channel_id=1, source_target_pairs={{0,496},{16,0},{32,16},{48,32},{64,48},{80,64},{96,80},{112,96},{1... | collective-permute-start | bytes 233288 | tf_op jit(solution)/shard_map/ppermute | solution.py:223
  2.7 3.8 %local_terms.1 = (f32[32,4,225]{2,1,0:T(4,128)S(1)}, f32[2,120,120]{2,1,0:T(8,128)S(1)}, bf16[120,81]{1,0:T(8,128)(2,1)S(1)}) custom-call(bf16[3,60,2,2916]{3,2,1,0:T(2,128)(2,1)} %bitcast.3, bf16[60,2,2916]{2,1,0:T(2,128)(2,1)} %bitcast.4, f32[2,2916]{1,0:T(2,128)} %pot.1, bf16[2,2,60,2,81]{4,3,2,1,0:T(2,128)(2,1)} %bitcast.6, f32[64]{0:T(128)} %penalty.1, ...), custom_call_target="tpu_custom_call" | custom-call | flops 400000000 | bytes 3000000 | tf_op jit(solution)/shard_map/local_terms/pallas_call | solution.py:243
  6.5 0.0 collective-permute-done.arrived
  6.5 0.4 %pair_terms.1 = f32[32,4,225]{2,1,0:T(4,128)S(1)} custom-call(bf16[2,2,60,2,81]{4,3,2,1,0:T(2,128)(2,1)S(1)} %collective-permute-done.arrived, bf16[120,81]{1,0:T(8,128)(2,1)S(1)} %get-tuple-element.8.edge, f32[2,120,120]{2,1,0:T(8,128)S(1)} %get-tuple-element.9.scales, f32[32,4,225]{2,1,0:T(4,128)S(1)} %get-tuple-element.10.chunks), custom_call_target="tpu_custom_call" | custom-call | tf_op jit(solution)/shard_map/pair_terms/pallas_call | solution.py:267
  6.9 24.8 %all_to_all.5.shared = f32[32,4,225]{2,1,0:T(4,128)S(1)} all-to-all(f32[32,4,225]{2,1,0:T(4,128)S(1)} %pair_terms.1), channel_id=1, replica_groups={{75,66,64,68,70,78,72,76,67,74,65,69,71,79,73,77,11,2,0,4,6,14,8,12,3,1..., dimensions={0} | all-to-all | bytes 230400 | tf_op jit(solution)/shard_map/all_to_all | solution.py:277
  31.7 0.6 %total_terms.1 = f32[2,2,225]{2,1,0:T(2,128)} custom-call(f32[32,4,225]{2,1,0:T(4,128)S(1)} %all_to_all.5.shared), custom_call_target="tpu_custom_call" | custom-call | tf_op jit(solution)/shard_map/total_terms/pallas_call | solution.py:278
Async XLA Ops:
  0.0 6.5 %collective-permute-start = (bf16[2,2,60,2,81]{4,3,2,1,0:T(2,128)(2,1)}, bf16[2,2,60,2,81]{4,3,2,1,0:T(2,128)(2,1)S(1)}, u32[]{:S(2)}, u32[]{:S(2)}) collective-permute-start(bf16[2,2,60,2,81]{4,3,2,1,0:T(2,128)(2,1)} %bitcast.5), channel_id=1, source_target_pairs={{0,496},{16,0},{32,16},{48,32},{64,48},{80,64},{96,80},{112,96},{1... | collective-permute-start | bytes 233288 | tf_op jit(solution)/shard_map/ppermute | solution.py:223

commit v8 on v5

--- a/solution.py
+++ b/solution.py
@@ -44,7 +44,7 @@
 
 
 def local_terms(grad, vals, pot, faces, penalty, orientation, chunks, scales, edge, grads, tiles, pots, sides,
-                pens, codes, stage, turned, blocks, sems):
+                pens, codes, stage, turned, blocks, lefts, sems):
     comps, width, count, points = grad.shape
     even = points // LANES * LANES
     rows = width * count
@@ -117,10 +117,14 @@
         level = jnp.where(odd[:, : tile.shape[1]], level[1:2], level[0:1])
         return (tile.astype(jnp.float32) * level * (1.0 / PTS)).astype(jnp.bfloat16)
 
-    tile = tiles[:, :even]
-    parts = [weighted(tile[:, at : at + LANES], pots[:, at : at + LANES]) for at in range(0, even, LANES)]
+    def weigh(step, carry):
+        lanes = pl.ds(pl.multiple_of(step * LANES, LANES), LANES)
+        lefts[:, lanes] = weighted(tiles[:, lanes], pots[:, lanes])
+        return carry
+
+    lax.fori_loop(0, even // LANES, weigh, 0)
     end = tiles[:, even:]
-    volume = gram(jnp.concatenate(parts, axis=1), tile) + gram(weighted(end, pots[:, even:]), end)
+    volume = gram(lefts[...], tiles[:, :even]) + gram(weighted(end, pots[:, even:]), end)
 
     masks = [(row == element) & (col == element) for element in range(count)]
     inner = 0.5 * (volume + volume.T)
@@ -256,6 +260,7 @@
             pltpu.SMEM(orientation.shape, jnp.int32),
             *fold_scratch,
             pltpu.VMEM((2 * count * width, width), jnp.float32),
+            pltpu.VMEM((rows, points // LANES * LANES), jnp.bfloat16),
             pltpu.SemaphoreType.DMA((comps + 5,)),
         ],
         compiler_params=pltpu.CompilerParams(vmem_limit_bytes=16 * MIB),

time: 32.2 us -> 32.3 us (level)
  transfers between devices with their start and end apart: 1 -> 1, of which waited for: 1 -> 1; matrix products, arithmetic and copies ran while one was open for 0% -> 0% of each run, Pallas kernels for 10% -> 11%
where the time goes in v8:
time: 32.3 us; the launch traced here: 32 us
  blocking collectives  24.5 us (76%)
  Pallas kernels  4.6 us (14%)
  starting transfers between devices  2.57 us (8%)
  waiting for transfers between devices  0.33 us (1%)
    all_to_all x1, blocking collectives, on_device(): lax.all_to_all(terms, ('elem', 'basis'), 0, 0, axis_index_groups=groups)  24.5 us
    pallas_call x1, Pallas kernels, on_device(): pl.pallas_call(local_terms, out_shape=[terms, pltpu.VMEM((2, rows, rows),...  3.6 us
    ppermute x1, starting transfers between devices, from_behind(): return lax.ppermute(value, axis, pairs)  2.57 us
  transfers between devices with their start and end apart: 1, of which 1 were waited for; matrix products, arithmetic and copies ran while one was open for 0% of the time, Pallas kernels for 11%

profile of v8, /device:TPU:15, one launch (start us, length us, event | category | flops | bytes accessed | tf_op | source)
XLA Modules:
  0.0 32.0 jit_solution(11194055708734324496)
XLA Ops:
  0.0 2.6 %collective-permute-start = (bf16[2,2,60,2,81]{4,3,2,1,0:T(2,128)(2,1)}, bf16[2,2,60,2,81]{4,3,2,1,0:T(2,128)(2,1)S(1)}, u32[]{:S(2)}, u32[]{:S(2)}) collective-permute-start(bf16[2,2,60,2,81]{4,3,2,1,0:T(2,128)(2,1)} %bitcast.5), channel_id=1, source_target_pairs={{0,496},{16,0},{32,16},{48,32},{64,48},{80,64},{96,80},{112,96},{1... | collective-permute-start | bytes 233288 | tf_op jit(solution)/shard_map/ppermute | solution.py:225
  2.6 3.6 %local_terms.1 = (f32[32,4,225]{2,1,0:T(4,128)S(1)}, f32[2,120,120]{2,1,0:T(8,128)S(1)}, bf16[120,81]{1,0:T(8,128)(2,1)S(1)}) custom-call(bf16[3,60,2,2916]{3,2,1,0:T(2,128)(2,1)} %bitcast.3, bf16[60,2,2916]{2,1,0:T(2,128)(2,1)} %bitcast.4, f32[2,2916]{1,0:T(2,128)} %pot.1, bf16[2,2,60,2,81]{4,3,2,1,0:T(2,128)(2,1)} %bitcast.6, f32[64]{0:T(128)} %penalty.1, ...), custom_call_target="tpu_custom_call" | custom-call | flops 400000000 | bytes 3000000 | tf_op jit(solution)/shard_map/local_terms/pallas_call | solution.py:245
  6.2 0.3 %collective-permute-done.arrived = bf16[2,2,60,2,81]{4,3,2,1,0:T(2,128)(2,1)S(1)} collective-permute-done((bf16[2,2,60,2,81]{4,3,2,1,0:T(2,128)(2,1)}, bf16[2,2,60,2,81]{4,3,2,1,0:T(2,128)(2,1)S(1)}, u32[]{:S(2)}, u32[]{:S(2)}) %collective-permute-start) | collective-permute-done | bytes 77792 | tf_op jit(solution)/shard_map/ppermute | solution.py:225
  6.5 0.4 %pair_terms.1 = f32[32,4,225]{2,1,0:T(4,128)S(1)} custom-call(bf16[2,2,60,2,81]{4,3,2,1,0:T(2,128)(2,1)S(1)} %collective-permute-done.arrived, bf16[120,81]{1,0:T(8,128)(2,1)S(1)} %get-tuple-element.8.edge, f32[2,120,120]{2,1,0:T(8,128)S(1)} %get-tuple-element.9.scales, f32[32,4,225]{2,1,0:T(4,128)S(1)} %get-tuple-element.10.chunks), custom_call_target="tpu_custom_call" | custom-call | tf_op jit(solution)/shard_map/pair_terms/pallas_call | solution.py:270
  6.9 24.5 %all_to_all.5.shared = f32[32,4,225]{2,1,0:T(4,128)S(1)} all-to-all(f32[32,4,225]{2,1,0:T(4,128)S(1)} %pair_terms.1), channel_id=1, replica_groups={{75,66,64,68,70,78,72,76,67,74,65,69,71,79,73,77,11,2,0,4,6,14,8,12,3,1..., dimensions={0} | all-to-all | bytes 230400 | tf_op jit(solution)/shard_map/all_to_all | solution.py:280
  31.4 0.6 %total_terms.1 = f32[2,2,225]{2,1,0:T(2,128)} custom-call(f32[32,4,225]{2,1,0:T(4,128)S(1)} %all_to_all.5.shared), custom_call_target="tpu_custom_call" | custom-call | tf_op jit(solution)/shard_map/total_terms/pallas_call | solution.py:281
Async XLA Ops:
  0.0 6.5 %collective-permute-start = (bf16[2,2,60,2,81]{4,3,2,1,0:T(2,128)(2,1)}, bf16[2,2,60,2,81]{4,3,2,1,0:T(2,128)(2,1)S(1)}, u32[]{:S(2)}, u32[]{:S(2)}) collective-permute-start(bf16[2,2,60,2,81]{4,3,2,1,0:T(2,128)(2,1)} %bitcast.5), channel_id=1, source_target_pairs={{0,496},{16,0},{32,16},{48,32},{64,48},{80,64},{96,80},{112,96},{1... | collective-permute-start | bytes 233288 | tf_op jit(solution)/shard_map/ppermute | solution.py:225

commit v9 on v5

--- a/solution.py
+++ b/solution.py
@@ -56,13 +56,11 @@
         )
     ]
 
-    def grad_move(comp):
-        return pltpu.make_async_copy(merged(grad).at[comp], grads.at[comp], sems.at[comp])
+    grad_move = pltpu.make_async_copy(merged(grad), grads, sems.at[0])
 
     for move in moves:
         move.start()
-    for comp in range(comps):
-        grad_move(comp).start()
+    grad_move.start()
     for move in moves[:3]:
         move.wait()
 
@@ -127,11 +125,11 @@
     steady = [jnp.where(mask, inner, 0.0) + part for mask, part in zip(masks, face_parts)]
 
     def add_comp(comp, kinetic):
-        grad_move(comp).wait()
         slope = grads[comp, :, :even]
         end = grads[comp, :, even:]
         return kinetic + gram(slope, slope) + gram(end, end)
 
+    grad_move.wait()
     kinetic = lax.fori_loop(0, comps, add_comp, jnp.zeros((rows, rows), jnp.float32))
     parts = [part + jnp.where(mask, (0.5 / PTS) * kinetic, 0.0) for part, mask in zip(steady, masks)]
     for element, diag in enumerate(fold(parts, stage, turned, width)):

time: 32.2 us -> 32.2 us (level)
  transfers between devices with their start and end apart: 1 -> 1, of which waited for: 1 -> 1; matrix products, arithmetic and copies ran while one was open for 0% -> 0% of each run, Pallas kernels for 10% -> 11%
where the time goes in v9:
time: 32.2 us; the launch traced here: 32 us
  blocking collectives  24.5 us (76%)
  Pallas kernels  4.41 us (14%)
  starting transfers between devices  2.57 us (8%)
  waiting for transfers between devices  0.52 us (2%)
    all_to_all x1, blocking collectives, on_device(): lax.all_to_all(terms, ('elem', 'basis'), 0, 0, axis_index_groups=groups)  24.5 us
    pallas_call x1, Pallas kernels, on_device(): pl.pallas_call(local_terms, out_shape=[terms, pltpu.VMEM((2, rows, rows),...  3.42 us
    ppermute x1, starting transfers between devices, from_behind(): return lax.ppermute(value, axis, pairs)  2.57 us
  transfers between devices with their start and end apart: 1, of which 1 were waited for; matrix products, arithmetic and copies ran while one was open for 0% of the time, Pallas kernels for 11%

profile of v9, /device:TPU:15, one launch (start us, length us, event | category | flops | bytes accessed | tf_op | source)
XLA Modules:
  0.0 32.0 jit_solution(13949758464593466830)
XLA Ops:
  0.0 2.6 %collective-permute-start = (bf16[2,2,60,2,81]{4,3,2,1,0:T(2,128)(2,1)}, bf16[2,2,60,2,81]{4,3,2,1,0:T(2,128)(2,1)S(1)}, u32[]{:S(2)}, u32[]{:S(2)}) collective-permute-start(bf16[2,2,60,2,81]{4,3,2,1,0:T(2,128)(2,1)} %bitcast.5), channel_id=1, source_target_pairs={{0,496},{16,0},{32,16},{48,32},{64,48},{80,64},{96,80},{112,96},{1... | collective-permute-start | bytes 233288 | tf_op jit(solution)/shard_map/ppermute | solution.py:219
  2.6 3.4 %local_terms.1 = (f32[32,4,225]{2,1,0:T(4,128)S(1)}, f32[2,120,120]{2,1,0:T(8,128)S(1)}, bf16[120,81]{1,0:T(8,128)(2,1)S(1)}) custom-call(bf16[3,60,2,2916]{3,2,1,0:T(2,128)(2,1)} %bitcast.3, bf16[60,2,2916]{2,1,0:T(2,128)(2,1)} %bitcast.4, f32[2,2916]{1,0:T(2,128)} %pot.1, bf16[2,2,60,2,81]{4,3,2,1,0:T(2,128)(2,1)} %bitcast.6, f32[64]{0:T(128)} %penalty.1, ...), custom_call_target="tpu_custom_call" | custom-call | flops 400000000 | bytes 3000000 | tf_op jit(solution)/shard_map/local_terms/pallas_call | solution.py:239
  6.0 0.5 %collective-permute-done.arrived = bf16[2,2,60,2,81]{4,3,2,1,0:T(2,128)(2,1)S(1)} collective-permute-done((bf16[2,2,60,2,81]{4,3,2,1,0:T(2,128)(2,1)}, bf16[2,2,60,2,81]{4,3,2,1,0:T(2,128)(2,1)S(1)}, u32[]{:S(2)}, u32[]{:S(2)}) %collective-permute-start) | collective-permute-done | bytes 77792 | tf_op jit(solution)/shard_map/ppermute | solution.py:219
  6.5 0.4 %pair_terms.1 = f32[32,4,225]{2,1,0:T(4,128)S(1)} custom-call(bf16[2,2,60,2,81]{4,3,2,1,0:T(2,128)(2,1)S(1)} %collective-permute-done.arrived, bf16[120,81]{1,0:T(8,128)(2,1)S(1)} %get-tuple-element.8.edge, f32[2,120,120]{2,1,0:T(8,128)S(1)} %get-tuple-element.9.scales, f32[32,4,225]{2,1,0:T(4,128)S(1)} %get-tuple-element.10.chunks), custom_call_target="tpu_custom_call" | custom-call | tf_op jit(solution)/shard_map/pair_terms/pallas_call | solution.py:263
  6.9 24.5 %all_to_all.5.shared = f32[32,4,225]{2,1,0:T(4,128)S(1)} all-to-all(f32[32,4,225]{2,1,0:T(4,128)S(1)} %pair_terms.1), channel_id=1, replica_groups={{75,66,64,68,70,78,72,76,67,74,65,69,71,79,73,77,11,2,0,4,6,14,8,12,3,1..., dimensions={0} | all-to-all | bytes 230400 | tf_op jit(solution)/shard_map/all_to_all | solution.py:273
  31.4 0.6 %total_terms.1 = f32[2,2,225]{2,1,0:T(2,128)} custom-call(f32[32,4,225]{2,1,0:T(4,128)S(1)} %all_to_all.5.shared), custom_call_target="tpu_custom_call" | custom-call | tf_op jit(solution)/shard_map/total_terms/pallas_call | solution.py:274
Async XLA Ops:
  0.0 6.5 %collective-permute-start = (bf16[2,2,60,2,81]{4,3,2,1,0:T(2,128)(2,1)}, bf16[2,2,60,2,81]{4,3,2,1,0:T(2,128)(2,1)S(1)}, u32[]{:S(2)}, u32[]{:S(2)}) collective-permute-start(bf16[2,2,60,2,81]{4,3,2,1,0:T(2,128)(2,1)} %bitcast.5), channel_id=1, source_target_pairs={{0,496},{16,0},{32,16},{48,32},{64,48},{80,64},{96,80},{112,96},{1... | collective-permute-start | bytes 233288 | tf_op jit(solution)/shard_map/ppermute | solution.py:219
